TPU v7x, 512 devices: a whole 4x4x16 slice. The times are simulated.
512 devices in a mesh: ctx: 32 (over y_hi, z), tp: 16 (over y_lo, x, core).
Axes of the slice: x: 4, y: 4 (y_hi: 2, y_lo: 2; y = y_hi * 2 + y_lo), z: 16, core: 2. Of those that a mesh axis runs over, the one named last changes fastest.
Arguments:
- query_rows: bfloat16 [4096, 1024], P('ctx', 'tp'), may hold values from -12 to 12
- key_rows: bfloat16 [4096, 1024], P('ctx', 'tp'), may hold values from -6 to 6
- value_rows: bfloat16 [4096, 1024], P('ctx', 'tp'), may hold values from -6 to 6
- valid_frames: int32 [1], replicated, may hold values from 3072 to 4096
- depth_kernel: float32 [32, 1024], P(None, 'tp'), may hold values from -1 to 1
- mix_weight: bfloat16 [1024, 1536], P('tp'), may hold values from -0.1875 to 0.1875
- out_grad: bfloat16 [4096, 1536], P(('ctx', 'tp')), may hold values from -6 to 6
Outputs:
- block_out: bfloat16 [4096, 1536], P(('ctx', 'tp'))
- query_grad: bfloat16 [4096, 1024], P('ctx', 'tp')
- key_grad: bfloat16 [4096, 1024], P('ctx', 'tp')
- value_grad: bfloat16 [4096, 1024], P('ctx', 'tp')
- mix_grad: float32 [1024, 1536], P('tp')
- kernel_grad: float32 [32, 1024], P(None, 'tp')
Inputs may be any that keep to these rules, and one draw needn't show every extreme that they name: Frames from valid_frames on are padding.
All inputs are finite; a program needn't handle non-finite values.
Results may differ from a plain program's by a relative error of at most 0.039.
Values may be sent and summed in bfloat16 or wider, within the bound.
No kernel may reach another device: no remote copies, remote signals or barrier semaphores. Data moves between devices by JAX's collectives and lax.ppermute only.
A program may use at most 64 MiB of HBM per device.

v0:
```python
import jax
import jax.numpy as jnp
from jax import lax
from jax.sharding import PartitionSpec as P

KSIZE = 32


def with_halo(block, sides, width):
    for axis, dim in sides:
        count = lax.axis_size(axis)
        forward = [(i, i + 1) for i in range(count - 1)]
        backward = [(target, source) for source, target in forward]
        low = lax.ppermute(
            lax.slice_in_dim(block, block.shape[dim] - width, None, axis=dim), axis, forward
        )
        high = lax.ppermute(lax.slice_in_dim(block, 0, width, axis=dim), axis, backward)
        block = jnp.concatenate([low, block, high], axis=dim)
    return block


def body(query_rows, key_rows, value_rows, valid_frames, depth_kernel, mix_weight, out_grad):
    frames_dev = query_rows.shape[0]
    head_width = query_rows.shape[1]
    score_scale = head_width ** (-0.5)
    total_frames = frames_dev * lax.axis_size("ctx")
    grad_norm = total_frames ** (-0.5)
    valid_count = valid_frames[0]
    own_ids = lax.axis_index("ctx") * frames_dev + jnp.arange(frames_dev, dtype=jnp.int32)
    own_live = own_ids < valid_count
    key_value = jnp.concatenate([key_rows, value_rows], axis=1)
    contract_last = (((1,), (1,)), ((), ()))
    key_piece = lax.all_gather(key_rows, "ctx", axis=0, tiled=True)
    run_max = jnp.full((frames_dev,), -1e30, jnp.float32)
    key_part = key_piece
    key_live = jnp.arange(key_piece.shape[0], dtype=jnp.int32) < valid_count
    scores = score_scale * lax.dot_general(
        query_rows, key_part, contract_last, preferred_element_type=jnp.float32
    )
    capped = jnp.where(key_live[None, :], scores, -1e30)
    new_max = jnp.maximum(run_max, jnp.max(capped, axis=1))
    weights = jnp.where(key_live[None, :], jnp.exp(capped - new_max[:, None]), 0.0)
    run_total = jnp.sum(weights, axis=1)
    run_max, run_total = (new_max, run_total)
    log_total = run_max + jnp.log(run_total)
    key_piece = lax.all_gather(key_value, "ctx", axis=0, tiled=True)
    key_part = key_piece[:, :head_width]
    value_part = key_piece[:, head_width:]
    key_live = jnp.arange(key_piece.shape[0], dtype=jnp.int32) < valid_count
    scores = score_scale * lax.dot_general(
        query_rows, key_part, contract_last, preferred_element_type=jnp.float32
    )
    capped = jnp.where(key_live[None, :], scores, -1e30)
    probs = jnp.where(key_live[None, :], jnp.exp(capped - log_total[:, None]), 0.0).astype(
        jnp.bfloat16
    )
    run_out = jnp.dot(probs, value_part, preferred_element_type=jnp.float32)
    attn = run_out.astype(jnp.bfloat16)
    masked = jnp.where(own_live[:, None], attn, jnp.zeros_like(attn))
    rim_width = KSIZE // 2
    padded_attn = with_halo(masked, (("ctx", 0),), rim_width)
    depth_out = jnp.zeros((frames_dev, head_width), jnp.float32)
    for offset in range(KSIZE):
        depth_out = depth_out + depth_kernel[offset][None, :] * padded_attn[
            offset : offset + frames_dev
        ].astype(jnp.float32)
    swished = (depth_out * jax.nn.sigmoid(depth_out)).astype(jnp.bfloat16)
    channel_rows = lax.all_to_all(swished, "tp", split_axis=0, concat_axis=1, tiled=True)
    full_weight = lax.all_gather(mix_weight, "tp", axis=0, tiled=True)
    block_out = jnp.dot(channel_rows, full_weight, preferred_element_type=jnp.float32).astype(
        jnp.bfloat16
    )
    grad_block = lax.all_gather(out_grad, "tp", axis=0, tiled=True)
    mix_back = lax.dot_general(
        grad_block, mix_weight, contract_last, preferred_element_type=jnp.float32
    )
    gate_sig = jax.nn.sigmoid(depth_out)
    depth_grad = (mix_back * gate_sig * (1.0 + depth_out * (1.0 - gate_sig))).astype(jnp.bfloat16)
    mix_part = lax.dot_general(
        swished, grad_block, (((0,), (0,)), ((), ())), preferred_element_type=jnp.float32
    )
    depth_grad_wide = depth_grad.astype(jnp.float32)
    kernel_rows = []
    for offset in range(KSIZE):
        kernel_rows.append(
            jnp.sum(
                padded_attn[offset : offset + frames_dev].astype(jnp.float32) * depth_grad_wide,
                axis=0,
            )
        )
    kernel_part = jnp.stack(kernel_rows, axis=0)
    mix_total, kernel_total = (
        lax.psum(mix_part.astype(jnp.bfloat16), "ctx").astype(jnp.float32),
        lax.psum(kernel_part.astype(jnp.bfloat16), "ctx").astype(jnp.float32),
    )
    mix_grad = grad_norm * mix_total
    kernel_grad = grad_norm * kernel_total
    padded_grad = with_halo(depth_grad, (("ctx", 0),), rim_width)
    back_sum = jnp.zeros((frames_dev, head_width), jnp.float32)
    for offset in range(KSIZE):
        first_row = 2 * rim_width - offset
        back_sum = back_sum + depth_kernel[offset][None, :] * padded_grad[
            first_row : first_row + frames_dev
        ].astype(jnp.float32)
    attn_grad = jnp.where(own_live[:, None], back_sum, jnp.zeros_like(back_sum)).astype(
        jnp.bfloat16
    )
    delta = jnp.sum(attn_grad.astype(jnp.float32) * attn.astype(jnp.float32), axis=1)
    key_piece = lax.all_gather(key_value, "ctx", axis=0, tiled=True)
    key_part = key_piece[:, :head_width]
    value_part = key_piece[:, head_width:]
    key_live = jnp.arange(key_piece.shape[0], dtype=jnp.int32) < valid_count
    scores = score_scale * lax.dot_general(
        query_rows, key_part, contract_last, preferred_element_type=jnp.float32
    )
    capped = jnp.where(key_live[None, :], scores, -1e30)
    weights = jnp.where(key_live[None, :], jnp.exp(capped - log_total[:, None]), 0.0)
    dprobs = lax.dot_general(
        attn_grad, value_part, contract_last, preferred_element_type=jnp.float32
    )
    dscores = (weights * (dprobs - delta[:, None])).astype(jnp.bfloat16)
    query_total = score_scale * jnp.dot(dscores, key_part, preferred_element_type=jnp.float32)
    query_grad = query_total.astype(jnp.bfloat16)
    query_and_grad = jnp.concatenate([query_rows, attn_grad], axis=1)
    row_stats = jnp.stack([log_total, delta], axis=1)
    all_stats = lax.all_gather(row_stats, "ctx", axis=0, tiled=True)
    rows_piece = lax.all_gather(query_and_grad, "ctx", axis=0, tiled=True)
    query_piece = rows_piece[:, :head_width]
    grad_piece = rows_piece[:, head_width:]
    total_piece = all_stats[:, 0]
    delta_piece = all_stats[:, 1]
    scores = score_scale * lax.dot_general(
        key_rows, query_piece, contract_last, preferred_element_type=jnp.float32
    )
    capped = jnp.where(own_live[:, None], scores, -1e30)
    weights = jnp.where(own_live[:, None], jnp.exp(capped - total_piece[None, :]), 0.0)
    dprobs = lax.dot_general(
        value_rows, grad_piece, contract_last, preferred_element_type=jnp.float32
    )
    dscores = (weights * (dprobs - delta_piece[None, :])).astype(jnp.bfloat16)
    key_total = score_scale * jnp.dot(dscores, query_piece, preferred_element_type=jnp.float32)
    value_total = jnp.dot(
        weights.astype(jnp.bfloat16), grad_piece, preferred_element_type=jnp.float32
    )
    key_total, value_total = (key_total, value_total)
    return (
        block_out,
        query_grad,
        key_total.astype(jnp.bfloat16),
        value_total.astype(jnp.bfloat16),
        mix_grad,
        kernel_grad,
    )


def solution(mesh):
    placed = (
        P("ctx", "tp"),
        P("ctx", "tp"),
        P("ctx", "tp"),
        P(),
        P(None, "tp"),
        P("tp", None),
        P(("ctx", "tp"), None),
    )
    return jax.shard_map(
        body,
        mesh=mesh,
        in_specs=placed,
        out_specs=(
            P(("ctx", "tp"), None),
            P("ctx", "tp"),
            P("ctx", "tp"),
            P("ctx", "tp"),
            P("tp", None),
            P(None, "tp"),
        ),
        check_vma=False,
    )
```

profile of v0, /device:TPU:1, one launch (start us, length us, event | category | flops | bytes accessed | tf_op | source)
XLA Modules:
  0.0 650.3 jit_solution(8706354773599395544)
XLA Ops:
  7.2 0.0 all-gather.4.cloned.1.call-start
  7.2 1.4 pad_maximum_fusion
  8.6 0.0 all-gather.4.cloned.1.call-update
  8.6 0.0 all-reduce.2.cloned.1.call-start
  9.3 72.7 %all_gather.20 = bf16[4096,64]{0,1:T(8,128)(2,1)S(1)} all-gather(bf16[128,64]{0,1:T(8,128)(2,1)} %param.8), channel_id=1, replica_groups=mesh['ctx'=32,'tp'=16] {'ctx'}, dimensions={0}, use_global_device_ids=true | all-gather | bytes 540672 | tf_op jit(solution)/shard_map/all_gather | solution.py:33
  82.1 1.3 fusion.177
  83.4 0.5 select_reduce_fusion
  84.0 58.7 %all-gather.4.cloned.1.call-done = bf16[4096,128]{0,1:T(8,128)(2,1)} async-done(((bf16[128,128]{0,1:T(8,128)(2,1)}), bf16[4096,128]{0,1:T(8,128)(2,1)}) %all-gather.4.cloned.1.call-update) | async-done | bytes 1048592 | tf_op jit(solution)/shard_map/all_gather | solution.py:46
  142.7 3.0 fusion.8
  145.7 0.3 broadcast_select_fusion
  146.0 0.1 fusion.176
  146.1 1.3 collective-permute-start.1
  147.4 4.0 collective-permute-start
  151.4 30.7 %all_gather.22 = bf16[128,1536]{1,0:T(8,128)(2,1)S(1)} all-gather(bf16[8,1536]{1,0:T(8,128)(2,1)S(1)} %copy-done.6), channel_id=1, replica_groups=mesh['ctx'=32,'tp'=16] {'tp'}, dimensions={0}, use_global_device_ids=true | all-gather | bytes 417792 | tf_op jit(solution)/shard_map/all_gather | solution.py:73
  182.1 0.6 multiply_convert_fusion
  182.7 0.5 fusion.97
  183.2 0.1 fusion.175
  183.3 2.9 collective-permute-start.3
  186.2 1.3 collective-permute-start.2
  187.5 0.9 convolution_convert_fusion
  188.4 0.0 all-reduce.2.cloned.1.call-update
  188.4 0.0 all-gather.8.cloned.1.call-start
  188.5 2.2 collective-permute-done.2
  190.7 0.6 multiply_reduce_fusion
  191.3 0.6 pad_maximum_fusion.1
  191.9 0.0 all-gather.6.cloned.1.call-start
  192.0 0.5 all-gather.6.cloned.1.call-update
  192.5 0.1 copy.13
  192.6 0.7 reshape.50
  193.3 4.9 all-to-all-start
  198.2 0.3 fusion.113
  198.6 0.4 fusion.98
  198.9 0.4 fusion.114
  199.3 0.1 stack.170
  199.5 62.3 %psum.15 = bf16[32,64]{1,0:T(8,128)(2,1)S(1)} all-reduce(bf16[32,64]{1,0:T(8,128)(2,1)S(1)} %stack.170), channel_id=1, replica_groups=mesh['ctx'=32,'tp'=16] {'ctx'}, use_global_device_ids=true, to_apply=%region_36.37 | all-reduce | flops 2048 | bytes 8192 | tf_op jit(solution)/shard_map/psum | solution.py:94
  261.8 0.6 convert_multiply_fusion.66
  262.4 58.0 %all_gather.24 = f32[4096,2]{0,1:T(2,128)S(1)} all-gather(f32[128,2]{0,1:T(2,128)S(1)} %pad_maximum_fusion.6), channel_id=1, replica_groups=mesh['ctx'=32,'tp'=16] {'ctx'}, dimensions={0}, use_global_device_ids=true | all-gather | bytes 33792 | tf_op jit(solution)/shard_map/all_gather | solution.py:126
  320.4 1.4 fusion.21
  321.9 0.1 reshape.51
  322.0 0.1 all_to_all.17
  322.1 127.2 %all-reduce.2.cloned.1.call-done = bf16[64,1536]{1,0:T(8,128)(2,1)} async-done(((bf16[64,1536]{1,0:T(8,128)(2,1)}), bf16[64,1536]{1,0:T(8,128)(2,1)}) %all-reduce.2.cloned.1.call-update) | async-done | bytes 196624 | tf_op jit(solution)/shard_map/psum | solution.py:93
  449.3 1.7 convert_multiply_fusion
  451.0 139.8 %all-gather.8.cloned.1.call-done = bf16[4096,128]{0,1:T(8,128)(2,1)} async-done(((bf16[128,128]{0,1:T(8,128)(2,1)}), bf16[4096,128]{0,1:T(8,128)(2,1)}) %all-gather.8.cloned.1.call-update) | async-done | bytes 1048592 | tf_op jit(solution)/shard_map/all_gather | solution.py:127
  590.8 2.1 fusion.11
  592.9 0.9 convolution_convert_fusion.2
  593.8 1.7 fusion.20
  595.5 45.2 %all-gather.6.cloned.1.call-done = bf16[1024,1536]{1,0:T(8,128)(2,1)} async-done(((bf16[64,1536]{1,0:T(8,128)(2,1)}), bf16[1024,1536]{1,0:T(8,128)(2,1)}) %all-gather.6.cloned.1.call-update) | async-done | bytes 3145744 | tf_op jit(solution)/shard_map/all_gather | solution.py:69
  640.7 3.0 convolution_convert_fusion.1
  (30 shorter events, 0.2 us)
Async XLA Ops:
  7.2 135.6 %all-gather.4.cloned.1.call-start = ((), (), s32[]{:S(2)}) async-start(), calls=%async_computation.1 | async-start | bytes 1081344 | tf_op jit(solution)/shard_map/all_gather | solution.py:46
  8.6 440.7 %all-reduce.2.cloned.1.call-start = ((), (), s32[]{:S(2)}) async-start(), calls=%async_computation.4 | async-start | bytes 393216 | tf_op jit(solution)/shard_map/psum | solution.py:93
  82.1 1.9 copy-start.7
  82.1 60.7 %copy-start.3 = (bf16[128,64]{0,1:T(8,128)(2,1)S(1)}, bf16[128,64]{0,1:T(8,128)(2,1)}, u32[]{:S(2)}) copy-start(bf16[128,64]{0,1:T(8,128)(2,1)} %param.7) | copy-start | bytes 49156
  142.7 3.0 copy-start.1
  145.7 5.7 copy-start.6
  145.7 37.0 %copy-start.2 = (bf16[64,1536]{1,0:T(8,128)(2,1)S(1)}, bf16[64,1536]{1,0:T(8,128)(2,1)}, u32[]{:S(2)}) copy-start(bf16[64,1536]{1,0:T(8,128)(2,1)} %param.12) | copy-start | bytes 589828
  146.1 36.0 %collective-permute-start.1 = (bf16[16,64]{0,1:T(8,128)(2,1)S(1)}, bf16[16,64]{0,1:T(8,128)(2,1)S(1)}, u32[]{:S(2)}, u32[]{:S(2)}) collective-permute-start(bf16[16,64]{0,1:T(8,128)(2,1)S(1)} %get-tuple-element.79), channel_id=1, source_target_pairs={{16,0},{32,16},{48,32},{64,48},{80,64},{96,80},{112,96},{128,112},... | collective-permute-start | bytes 6152 | tf_op jit(solution)/shard_map/ppermute | solution.py:17
  147.4 34.7 %collective-permute-start = (bf16[16,64]{0,1:T(8,128)(2,1)S(1)}, bf16[16,64]{0,1:T(8,128)(2,1)S(1)}, u32[]{:S(2)}, u32[]{:S(2)}) collective-permute-start(bf16[16,64]{0,1:T(8,128)(2,1)S(1)} %get-tuple-element.78), channel_id=1, source_target_pairs={{0,16},{16,32},{32,48},{48,64},{64,80},{80,96},{96,112},{112,128},... | collective-permute-start | bytes 6152 | tf_op jit(solution)/shard_map/ppermute | solution.py:14
  183.3 5.2 collective-permute-start.3
  186.2 4.5 collective-permute-start.2
  188.4 402.4 %all-gather.8.cloned.1.call-start = ((), (), s32[]{:S(2)}) async-start(), calls=%async_computation.3 | async-start | bytes 1081344 | tf_op jit(solution)/shard_map/all_gather | solution.py:127
  191.9 448.8 %all-gather.6.cloned.1.call-start = ((), (), s32[]{:S(2)}) async-start(), calls=%async_computation.2 | async-start | bytes 3342336 | tf_op jit(solution)/shard_map/all_gather | solution.py:69
  193.3 128.5 %all-to-all-start = ((bf16[16,2,256]{2,1,0:T(2,128)(2,1)}), bf16[16,2,256]{2,1,0:T(2,128)(2,1)S(1)}, u32[]{:S(2)}, u32[]{:S(2)}) async-start(bf16[16,2,256]{2,1,0:T(2,128)(2,1)} %reshape.50), calls=%async_computation | async-start | bytes 32768 | tf_op jit(solution)/shard_map/all_to_all | solution.py:68
  199.3 391.5 %copy-start.5 = (bf16[128,64]{0,1:T(8,128)(2,1)S(1)}, bf16[128,64]{0,1:T(8,128)(2,1)}, u32[]{:S(2)}) copy-start(bf16[128,64]{0,1:T(8,128)(2,1)} %param.8) | copy-start | bytes 49156
  590.8 2.1 copy-start
  592.9 0.9 copy-start.4
Sparse Core Ops, SparseCore 0:
  11.5 131.2 all-gather.3
  188.5 260.7 all-reduce.1
  452.6 138.1 all-gather.7
  593.0 47.6 all-gather.5
where the time goes:
time: 651 us; the launch traced here: 650 us
  waiting for transfers between devices  374 us (57%)
  blocking collectives  224 us (34%)
  matrix products  15 us (2%)
  between operations  14.6 us (2%)
  starting transfers between devices  14.5 us (2%)
  other arithmetic  7.18 us (1%)
    all_gather x1, waiting for transfers between devices, body(): rows_piece = lax.all_gather(query_and_grad, 'ctx', axis=0, tiled=True)  140 us
    psum x1, waiting for transfers between devices, body(): lax.psum(mix_part.astype(jnp.bfloat16), 'ctx').astype(jnp.float32)  127 us
    all_gather x1, blocking collectives, body(): key_piece = lax.all_gather(key_rows, 'ctx', axis=0, tiled=True)  72.7 us
    psum x1, blocking collectives, body(): lax.psum(kernel_part.astype(jnp.bfloat16), 'ctx').astype(jnp.float32)  62.3 us
    all_gather x1, waiting for transfers between devices, body(): key_piece = lax.all_gather(key_value, 'ctx', axis=0, tiled=True)  58.7 us
    all_gather x1, blocking collectives, body(): all_stats = lax.all_gather(row_stats, 'ctx', axis=0, tiled=True)  58 us
    all_gather x1, waiting for transfers between devices, body(): full_weight = lax.all_gather(mix_weight, 'tp', axis=0, tiled=True)  45.2 us
    all_gather x1, blocking collectives, body(): grad_block = lax.all_gather(out_grad, 'tp', axis=0, tiled=True)  30.7 us
  transfers between devices with their start and end apart: 9, of which 5 were waited for; matrix products, arithmetic and copies ran while one was open for 2% of the time, Pallas kernels for 0%

commit v1 on v0

--- a/solution.py
+++ b/solution.py
@@ -123,8 +123,13 @@
     query_grad = query_total.astype(jnp.bfloat16)
     query_and_grad = jnp.concatenate([query_rows, attn_grad], axis=1)
     row_stats = jnp.stack([log_total, delta], axis=1)
-    all_stats = lax.all_gather(row_stats, "ctx", axis=0, tiled=True)
-    rows_piece = lax.all_gather(query_and_grad, "ctx", axis=0, tiled=True)
+    all_stats, rows_piece = jnp.split(
+        lax.all_gather(
+            jnp.concatenate([row_stats, query_and_grad], axis=1), "ctx", axis=0, tiled=True
+        ),
+        [row_stats.shape[1]],
+        axis=1,
+    )
     query_piece = rows_piece[:, :head_width]
     grad_piece = rows_piece[:, head_width:]
     total_piece = all_stats[:, 0]

time: 651 us -> 488 us (0.75)
  the two profiles are of different devices: /device:TPU:1 before, /device:TPU:2 now
where the time goes in v1:
time: 488 us; the launch traced here: 487 us
  waiting for transfers between devices  235 us (48%)
  blocking collectives  178 us (36%)
  matrix products  20.2 us (4%)
  between operations  16.8 us (3%)
  starting transfers between devices  16.5 us (3%)
  other arithmetic  13.2 us (3%)
  local copies, waits for them, and re-layouts  7.07 us (1%)
    psum x1, waiting for transfers between devices, body(): lax.psum(mix_part.astype(jnp.bfloat16), 'ctx').astype(jnp.float32)  176 us
    all_gather x1, blocking collectives, body(): key_piece = lax.all_gather(key_rows, 'ctx', axis=0, tiled=True)  85.7 us
    psum x1, blocking collectives, body(): lax.psum(kernel_part.astype(jnp.bfloat16), 'ctx').astype(jnp.float32)  75.3 us
    all_gather x1, waiting for transfers between devices, body(): key_piece = lax.all_gather(key_value, 'ctx', axis=0, tiled=True)  53.6 us
    all_gather x1, blocking collectives, body(): grad_block = lax.all_gather(out_grad, 'tp', axis=0, tiled=True)  17.6 us
  transfers between devices with their start and end apart: 9, of which 4 were waited for; matrix products, arithmetic and copies ran while one was open for 5% of the time, Pallas kernels for 0%

profile of v1, /device:TPU:2, one launch (start us, length us, event | category | flops | bytes accessed | tf_op | source)
XLA Modules:
  0.0 487.0 jit_solution(9355999363535936008)
XLA Ops:
  8.0 1.4 pad_maximum_fusion.1
  9.4 0.0 all-reduce.2.cloned.1.call-start
  10.2 85.7 %all_gather.17 = bf16[4096,64]{0,1:T(8,128)(2,1)S(1)} all-gather(bf16[128,64]{0,1:T(8,128)(2,1)} %param.8), channel_id=1, replica_groups=mesh['ctx'=32,'tp'=16] {'ctx'}, dimensions={0}, use_global_device_ids=true | all-gather | bytes 540672 | tf_op jit(solution)/shard_map/all_gather | solution.py:33
  95.8 1.3 fusion.177
  97.2 0.5 select_reduce_fusion
  97.8 0.6 slice_bitcast_fusion.30
  98.4 0.7 slice_bitcast_fusion.31
  99.1 53.6 %all-gather.4.cloned.1.call-done = bf16[4096,128]{0,1:T(8,128)(2,1)} async-done(((bf16[128,128]{0,1:T(8,128)(2,1)}), bf16[4096,128]{0,1:T(8,128)(2,1)}) %all-gather.4.cloned.1.call-update) | async-done | bytes 1048592 | tf_op jit(solution)/shard_map/all_gather | solution.py:46
  152.7 3.0 fusion.11
  156.0 0.9 broadcast_select_fusion
  156.9 0.1 fusion.176
  157.0 1.3 collective-permute-start.1
  158.3 4.5 collective-permute-start
  162.8 17.6 %all_gather.19 = bf16[128,1536]{1,0:T(8,128)(2,1)S(1)} all-gather(bf16[8,1536]{1,0:T(8,128)(2,1)S(1)} %copy-done.8), channel_id=1, replica_groups=mesh['ctx'=32,'tp'=16] {'tp'}, dimensions={0}, use_global_device_ids=true | all-gather | bytes 417792 | tf_op jit(solution)/shard_map/all_gather | solution.py:73
  180.4 0.6 copy-done.3
  181.3 1.3 multiply_convert_fusion
  182.6 0.6 copy-done.2
  183.2 0.9 convolution_convert_fusion
  184.1 0.0 all-gather.6.cloned.1.call-start
  184.1 0.5 all-gather.6.cloned.1.call-update
  184.7 2.1 fusion.97
  186.8 0.1 fusion.175
  186.9 3.2 collective-permute-start.3
  190.1 1.3 collective-permute-start.2
  191.4 0.1 collective-permute-done.3
  191.5 4.2 collective-permute-done.2
  195.7 1.4 multiply_reduce_fusion
  197.2 0.7 maximum_convert_fusion
  197.9 1.3 pad_maximum_fusion
  199.2 0.8 copy.13
  200.1 0.7 reshape.50
  200.8 6.1 %all-to-all-start = ((bf16[16,2,256]{2,1,0:T(2,128)(2,1)}), bf16[16,2,256]{2,1,0:T(2,128)(2,1)S(1)}, u32[]{:S(2)}, u32[]{:S(2)}) async-start(bf16[16,2,256]{2,1,0:T(2,128)(2,1)} %reshape.50), calls=%async_computation | async-start | bytes 32768 | tf_op jit(solution)/shard_map/all_to_all | solution.py:68
  206.8 1.3 fusion.113
  208.1 1.5 fusion.98
  209.6 1.5 fusion.114
  211.0 1.5 stack.166
  212.5 75.3 %psum.15 = bf16[32,64]{1,0:T(8,128)(2,1)S(1)} all-reduce(bf16[32,64]{1,0:T(8,128)(2,1)S(1)} %stack.166), channel_id=1, replica_groups=mesh['ctx'=32,'tp'=16] {'ctx'}, use_global_device_ids=true, to_apply=%region_36.37 | all-reduce | flops 2048 | bytes 8192 | tf_op jit(solution)/shard_map/psum | solution.py:94
  287.8 0.6 convert_multiply_fusion.66
  288.4 1.4 fusion.20
  289.9 0.1 reshape.51
  290.0 0.1 all_to_all.17
  290.1 176.2 %all-reduce.2.cloned.1.call-done = bf16[64,1536]{1,0:T(8,128)(2,1)} async-done(((bf16[64,1536]{1,0:T(8,128)(2,1)}), bf16[64,1536]{1,0:T(8,128)(2,1)}) %all-reduce.2.cloned.1.call-update) | async-done | bytes 196624 | tf_op jit(solution)/shard_map/psum | solution.py:93
  466.2 1.7 convert_multiply_fusion
  467.9 3.0 convolution_convert_fusion.1
  470.9 1.0 fusion.174
  472.0 2.1 fusion.4
  474.1 2.2 convolution_convert_fusion.3
  476.3 3.3 fusion.21
  (103 shorter events, 0.4 us)
Async XLA Ops:
  8.0 144.7 %all-gather.4.cloned.1.call-start = ((), (), s32[]{:S(2)}) async-start(), calls=%async_computation.1 | async-start | bytes 1081344 | tf_op jit(solution)/shard_map/all_gather | solution.py:46
  9.4 456.8 %all-reduce.2.cloned.1.call-start = ((), (), s32[]{:S(2)}) async-start(), calls=%async_computation.4 | async-start | bytes 393216 | tf_op jit(solution)/shard_map/psum | solution.py:93
  10.1 145.5 %copy-start.42 = (pred[128]{0:T(512)(128)(4,1)}, pred[128]{0:T(512)(128)(4,1)S(1)}, u32[]{:S(2)}) copy-start(pred[128]{0:T(512)(128)(4,1)S(1)} %add_compare_fusion) | copy-start | bytes 388
  95.8 56.8 %copy-start.4 = (bf16[128,64]{0,1:T(8,128)(2,1)S(1)}, bf16[128,64]{0,1:T(8,128)(2,1)}, u32[]{:S(2)}) copy-start(bf16[128,64]{0,1:T(8,128)(2,1)} %param.7) | copy-start | bytes 49156
  97.7 57.9 %copy-start.44 = (f32[128]{0:T(128)}, f32[128]{0:T(128)S(1)}, u32[]{:S(2)}) copy-start(f32[128]{0:T(128)S(1)} %log_add_fusion) | copy-start | bytes 1540
  155.7 7.2 %copy-start.8 = (bf16[8,1536]{1,0:T(8,128)(2,1)S(1)}, bf16[8,1536]{1,0:T(8,128)(2,1)}, u32[]{:S(2)}) copy-start(bf16[8,1536]{1,0:T(8,128)(2,1)} %param.13) | copy-start | bytes 73732
  155.7 25.3 %copy-start.10 = (f32[64]{0:T(128)S(1)}, f32[64]{0:T(128)}, u32[]{:S(2)}) copy-start(f32[64]{0:T(128)} %get-tuple-element.46) | copy-start | bytes 772
  155.7 25.3 %copy-start.11 = (f32[64]{0:T(128)S(1)}, f32[64]{0:T(128)}, u32[]{:S(2)}) copy-start(f32[64]{0:T(128)} %get-tuple-element.47) | copy-start | bytes 772
  155.7 25.3 %copy-start.12 = (f32[64]{0:T(128)S(1)}, f32[64]{0:T(128)}, u32[]{:S(2)}) copy-start(f32[64]{0:T(128)} %get-tuple-element.48) | copy-start | bytes 772
  155.7 25.3 %copy-start.13 = (f32[64]{0:T(128)S(1)}, f32[64]{0:T(128)}, u32[]{:S(2)}) copy-start(f32[64]{0:T(128)} %get-tuple-element.49) | copy-start | bytes 772
  155.7 25.3 %copy-start.14 = (f32[64]{0:T(128)S(1)}, f32[64]{0:T(128)}, u32[]{:S(2)}) copy-start(f32[64]{0:T(128)} %get-tuple-element.50) | copy-start | bytes 772
  155.7 25.3 %copy-start.15 = (f32[64]{0:T(128)S(1)}, f32[64]{0:T(128)}, u32[]{:S(2)}) copy-start(f32[64]{0:T(128)} %get-tuple-element.51) | copy-start | bytes 772
  155.7 25.3 %copy-start.16 = (f32[64]{0:T(128)S(1)}, f32[64]{0:T(128)}, u32[]{:S(2)}) copy-start(f32[64]{0:T(128)} %get-tuple-element.52) | copy-start | bytes 772
  155.8 25.3 %copy-start.17 = (f32[64]{0:T(128)S(1)}, f32[64]{0:T(128)}, u32[]{:S(2)}) copy-start(f32[64]{0:T(128)} %get-tuple-element.53) | copy-start | bytes 772
  155.8 25.3 %copy-start.18 = (f32[64]{0:T(128)S(1)}, f32[64]{0:T(128)}, u32[]{:S(2)}) copy-start(f32[64]{0:T(128)} %get-tuple-element.54) | copy-start | bytes 772
  155.8 25.3 %copy-start.19 = (f32[64]{0:T(128)S(1)}, f32[64]{0:T(128)}, u32[]{:S(2)}) copy-start(f32[64]{0:T(128)} %get-tuple-element.55) | copy-start | bytes 772
  155.8 25.3 %copy-start.20 = (f32[64]{0:T(128)S(1)}, f32[64]{0:T(128)}, u32[]{:S(2)}) copy-start(f32[64]{0:T(128)} %get-tuple-element.56) | copy-start | bytes 772
  155.8 25.3 %copy-start.21 = (f32[64]{0:T(128)S(1)}, f32[64]{0:T(128)}, u32[]{:S(2)}) copy-start(f32[64]{0:T(128)} %get-tuple-element.57) | copy-start | bytes 772
  155.8 25.3 %copy-start.22 = (f32[64]{0:T(128)S(1)}, f32[64]{0:T(128)}, u32[]{:S(2)}) copy-start(f32[64]{0:T(128)} %get-tuple-element.58) | copy-start | bytes 772
  155.8 25.3 %copy-start.23 = (f32[64]{0:T(128)S(1)}, f32[64]{0:T(128)}, u32[]{:S(2)}) copy-start(f32[64]{0:T(128)} %get-tuple-element.59) | copy-start | bytes 772
  155.8 25.3 %copy-start.24 = (f32[64]{0:T(128)S(1)}, f32[64]{0:T(128)}, u32[]{:S(2)}) copy-start(f32[64]{0:T(128)} %get-tuple-element.60) | copy-start | bytes 772
  155.8 25.3 %copy-start.25 = (f32[64]{0:T(128)S(1)}, f32[64]{0:T(128)}, u32[]{:S(2)}) copy-start(f32[64]{0:T(128)} %get-tuple-element.61) | copy-start | bytes 772
  155.8 25.3 %copy-start.26 = (f32[64]{0:T(128)S(1)}, f32[64]{0:T(128)}, u32[]{:S(2)}) copy-start(f32[64]{0:T(128)} %get-tuple-element.62) | copy-start | bytes 772
  155.9 25.3 %copy-start.27 = (f32[64]{0:T(128)S(1)}, f32[64]{0:T(128)}, u32[]{:S(2)}) copy-start(f32[64]{0:T(128)} %get-tuple-element.63) | copy-start | bytes 772
  155.9 25.3 %copy-start.28 = (f32[64]{0:T(128)S(1)}, f32[64]{0:T(128)}, u32[]{:S(2)}) copy-start(f32[64]{0:T(128)} %get-tuple-element.64) | copy-start | bytes 772
  155.9 25.3 %copy-start.29 = (f32[64]{0:T(128)S(1)}, f32[64]{0:T(128)}, u32[]{:S(2)}) copy-start(f32[64]{0:T(128)} %get-tuple-element.65) | copy-start | bytes 772
  155.9 25.3 %copy-start.30 = (f32[64]{0:T(128)S(1)}, f32[64]{0:T(128)}, u32[]{:S(2)}) copy-start(f32[64]{0:T(128)} %get-tuple-element.66) | copy-start | bytes 772
  155.9 25.3 %copy-start.31 = (f32[64]{0:T(128)S(1)}, f32[64]{0:T(128)}, u32[]{:S(2)}) copy-start(f32[64]{0:T(128)} %get-tuple-element.67) | copy-start | bytes 772
  155.9 25.3 %copy-start.32 = (f32[64]{0:T(128)S(1)}, f32[64]{0:T(128)}, u32[]{:S(2)}) copy-start(f32[64]{0:T(128)} %get-tuple-element.68) | copy-start | bytes 772
  155.9 25.3 %copy-start.33 = (f32[64]{0:T(128)S(1)}, f32[64]{0:T(128)}, u32[]{:S(2)}) copy-start(f32[64]{0:T(128)} %get-tuple-element.69) | copy-start | bytes 772
  155.9 25.3 %copy-start.34 = (f32[64]{0:T(128)S(1)}, f32[64]{0:T(128)}, u32[]{:S(2)}) copy-start(f32[64]{0:T(128)} %get-tuple-element.70) | copy-start | bytes 772
  155.9 25.3 %copy-start.35 = (f32[64]{0:T(128)S(1)}, f32[64]{0:T(128)}, u32[]{:S(2)}) copy-start(f32[64]{0:T(128)} %get-tuple-element.71) | copy-start | bytes 772
  155.9 25.3 %copy-start.36 = (f32[64]{0:T(128)S(1)}, f32[64]{0:T(128)}, u32[]{:S(2)}) copy-start(f32[64]{0:T(128)} %get-tuple-element.72) | copy-start | bytes 772
  156.0 25.3 %copy-start.37 = (f32[64]{0:T(128)S(1)}, f32[64]{0:T(128)}, u32[]{:S(2)}) copy-start(f32[64]{0:T(128)} %get-tuple-element.73) | copy-start | bytes 772
  156.0 25.3 %copy-start.38 = (f32[64]{0:T(128)S(1)}, f32[64]{0:T(128)}, u32[]{:S(2)}) copy-start(f32[64]{0:T(128)} %get-tuple-element.74) | copy-start | bytes 772
  156.0 25.3 %copy-start.39 = (f32[64]{0:T(128)S(1)}, f32[64]{0:T(128)}, u32[]{:S(2)}) copy-start(f32[64]{0:T(128)} %get-tuple-element.75) | copy-start | bytes 772
  156.0 25.3 %copy-start.40 = (f32[64]{0:T(128)S(1)}, f32[64]{0:T(128)}, u32[]{:S(2)}) copy-start(f32[64]{0:T(128)} %get-tuple-element.76) | copy-start | bytes 772
  156.0 25.3 %copy-start.41 = (f32[64]{0:T(128)S(1)}, f32[64]{0:T(128)}, u32[]{:S(2)}) copy-start(f32[64]{0:T(128)} %get-tuple-element.77) | copy-start | bytes 772
  157.0 23.4 %collective-permute-start.1 = (bf16[16,64]{0,1:T(8,128)(2,1)S(1)}, bf16[16,64]{0,1:T(8,128)(2,1)S(1)}, u32[]{:S(2)}, u32[]{:S(2)}) collective-permute-start(bf16[16,64]{0,1:T(8,128)(2,1)S(1)} %get-tuple-element.79), channel_id=1, source_target_pairs={{16,0},{32,16},{48,32},{64,48},{80,64},{96,80},{112,96},{128,112},... | collective-permute-start | bytes 6152 | tf_op jit(solution)/shard_map/ppermute | solution.py:17
  158.3 22.1 %collective-permute-start = (bf16[16,64]{0,1:T(8,128)(2,1)S(1)}, bf16[16,64]{0,1:T(8,128)(2,1)S(1)}, u32[]{:S(2)}, u32[]{:S(2)}) collective-permute-start(bf16[16,64]{0,1:T(8,128)(2,1)S(1)} %get-tuple-element.78), channel_id=1, source_target_pairs={{0,16},{16,32},{32,48},{48,64},{64,80},{80,96},{96,112},{112,128},... | collective-permute-start | bytes 6152 | tf_op jit(solution)/shard_map/ppermute | solution.py:14
  184.1 283.9 %all-gather.6.cloned.1.call-start = ((), (), s32[]{:S(2)}) async-start(), calls=%async_computation.2 | async-start | bytes 3342336 | tf_op jit(solution)/shard_map/all_gather | solution.py:69
  184.6 286.3 %all-gather.8.cloned.1.call-start = ((), (), s32[]{:S(2)}) async-start(), calls=%async_computation.3 | async-start | bytes 2297856 | tf_op jit(solution)/shard_map/all_gather | solution.py:127
  186.8 8.9 %copy-start.1 = (bf16[128,64]{0,1:T(8,128)(2,1)}, bf16[128,64]{0,1:T(8,128)(2,1)S(1)}, u32[]{:S(2)}) copy-start(bf16[128,64]{0,1:T(8,128)(2,1)S(1)} %get-tuple-element.84) | copy-start | bytes 49156
  186.9 4.6 collective-permute-start.3
  190.1 5.6 %collective-permute-start.2 = (bf16[16,64]{0,1:T(8,128)(2,1)S(1)}, bf16[16,64]{0,1:T(8,128)(2,1)S(1)}, u32[]{:S(2)}, u32[]{:S(2)}) collective-permute-start(bf16[16,64]{0,1:T(8,128)(2,1)S(1)} %get-tuple-element.44), channel_id=1, source_target_pairs={{16,0},{32,16},{48,32},{64,48},{80,64},{96,80},{112,96},{128,112},... | collective-permute-start | bytes 6152 | tf_op jit(solution)/shard_map/ppermute | solution.py:17
  200.8 89.1 %all-to-all-start = ((bf16[16,2,256]{2,1,0:T(2,128)(2,1)}), bf16[16,2,256]{2,1,0:T(2,128)(2,1)S(1)}, u32[]{:S(2)}, u32[]{:S(2)}) async-start(bf16[16,2,256]{2,1,0:T(2,128)(2,1)} %reshape.50), calls=%async_computation | async-start | bytes 32768 | tf_op jit(solution)/shard_map/all_to_all | solution.py:68
  289.9 182.1 %copy-start.7 = (bf16[128,64]{0,1:T(8,128)(2,1)S(1)}, bf16[128,64]{0,1:T(8,128)(2,1)}, u32[]{:S(2)}) copy-start(bf16[128,64]{0,1:T(8,128)(2,1)} %param.8) | copy-start | bytes 49156
  289.9 182.1 %copy-start.43 = (pred[128]{0:T(512)(128)(4,1)S(1)}, pred[128]{0:T(512)(128)(4,1)}, u32[]{:S(2)}) copy-start(pred[128]{0:T(512)(128)(4,1)} %copy-done.42) | copy-start | bytes 388
  (6 other events, 10.4 us)
Sparse Core Ops, SparseCore 0:
  12.3 140.3 all-gather.3
  184.2 281.9 all-reduce.1
Sparse Core Ops, SparseCore 1:
  186.7 38.8 all-gather.5
  228.3 148.8 all-gather.7
